TPU v7x, 32 devices: a whole 2x2x4 slice. The times are simulated.
32 devices in a mesh: img: 2 (over x), row: 4 (over z), col: 4 (over y, core).
Axes of the slice: x: 2, y: 2, z: 4, core: 2. Of those that a mesh axis runs over, the one named last changes fastest.
Arguments:
- latent: bfloat16 [128, 64, 1280], P(('img', 'row'), 'col'), parts along dimension 0, may hold values from -240 to 240
- norm_gain: float32 [1280], replicated, may hold values from 0.1 to 1.9
- norm_shift: float32 [1280], replicated, may hold values from -3 to 3
- query_weight: bfloat16 [1280, 768], replicated, may hold values from -0.25 to 0.25
- key_weight: bfloat16 [1280, 768], replicated, may hold values from -0.25 to 0.25
- value_weight: bfloat16 [1280, 768], replicated, may hold values from -0.15625 to 0.15625
- output_weight: bfloat16 [768, 1280], replicated, may hold values from -0.875 to 0.875
- output_bias: float32 [1280], replicated, may hold values from -3 to 3
Outputs:
- attended: bfloat16 [128, 64, 1280], P(('img', 'row'), 'col'), parts along dimension 0
There are 2 independent parts, one for each index of `img`. A program takes and returns all parts, laid end to end along the dimension named above; an argument that names none is the same for every part. Nothing has to cross between parts.
All inputs are finite; a program needn't handle non-finite values.
Results may differ from a plain program's by a relative error of at most 0.012.
The roundings to bfloat16 on the way count: a program that leaves them out, or rounds other values in their place, can miss the bound.
Values may be sent and summed in bfloat16 or wider, within the bound.
A program may use at most 128 MiB of HBM per device.

v0:
```python
import math
import jax
import jax.numpy as jnp
from jax import lax
from jax.sharding import PartitionSpec as P

GROUPS = 32
HD = 64


def attend(carry, piece, queries):
    keys, values = piece
    heads_here = queries.shape[1] // HD
    scale = 1.0 / math.sqrt(HD)
    query_heads = queries.reshape(queries.shape[0], heads_here, HD).transpose(1, 0, 2)
    key_heads = keys.reshape(keys.shape[0], heads_here, HD).transpose(1, 0, 2)
    value_heads = values.reshape(values.shape[0], heads_here, HD).transpose(1, 0, 2)

    def per_head(items):
        query_one, key_one, value_one, peak_old, total_old, mixed_old = items
        scores = jnp.dot(query_one, key_one.T, preferred_element_type=jnp.float32) * scale
        peak_new = jnp.maximum(peak_old, jnp.max(scores, axis=1))
        factor = jnp.exp(peak_old - peak_new)
        weights = jnp.exp(scores - peak_new[:, None])
        total_new = total_old * factor + jnp.sum(weights, axis=1)
        rounded = weights.astype(jnp.bfloat16)
        mixed_new = mixed_old * factor[:, None] + jnp.dot(
            rounded, value_one, preferred_element_type=jnp.float32
        )
        return (peak_new, total_new, mixed_new)

    return lax.map(per_head, (query_heads, key_heads, value_heads) + tuple(carry))


def start_state(queries):
    heads_here = queries.shape[1] // HD
    count = queries.shape[0]
    peak = jnp.full((heads_here, count), -1e30, jnp.float32)
    total = jnp.zeros((heads_here, count), jnp.float32)
    mixed = jnp.zeros((heads_here, count, HD), jnp.float32)
    return (peak, total, mixed)


def finish(state):
    peak, total, mixed = state
    heads_here, count, _ = mixed.shape
    result = mixed / total[:, :, None]
    return result.transpose(1, 0, 2).reshape(count, heads_here * HD).astype(jnp.bfloat16)


def local(
    latent,
    norm_gain,
    norm_shift,
    query_weight,
    key_weight,
    value_weight,
    output_weight,
    output_bias,
):
    rows_here, cols_here, width = latent.shape
    tok_count = rows_here * cols_here
    wide = latent.reshape(tok_count, width).astype(jnp.float32)
    grouped = wide.reshape(tok_count, GROUPS, width // GROUPS)
    entries = float(tok_count * lax.axis_size("row") * lax.axis_size("col") * (width // GROUPS))
    group_total = lax.psum(jnp.sum(grouped, axis=(0, 2)), ("row", "col"))
    mean = group_total / entries
    centered = grouped - mean[None, :, None]
    spread = lax.psum(jnp.sum(centered * centered, axis=(0, 2)), ("row", "col"))
    variance = spread / entries
    scaled = (centered * lax.rsqrt(variance + 1e-05)[None, :, None]).reshape(tok_count, width)
    normed = (scaled * norm_gain + norm_shift).astype(jnp.bfloat16)
    queries = jnp.dot(normed, query_weight, preferred_element_type=jnp.float32).astype(jnp.bfloat16)
    keys = jnp.dot(normed, key_weight, preferred_element_type=jnp.float32).astype(jnp.bfloat16)
    values = jnp.dot(normed, value_weight, preferred_element_type=jnp.float32).astype(jnp.bfloat16)
    state = attend(
        start_state(queries),
        (
            lax.all_gather(keys, ("row", "col"), axis=0, tiled=True),
            lax.all_gather(values, ("row", "col"), axis=0, tiled=True),
        ),
        queries,
    )
    mixed = finish(state)
    result = jnp.dot(mixed, output_weight, preferred_element_type=jnp.float32) + output_bias
    return result.astype(jnp.bfloat16).reshape(rows_here, cols_here, width)


def solution(mesh):
    placed = (P(("img", "row"), "col", None), P(), P(), P(), P(), P(), P(), P())
    return jax.shard_map(
        local, mesh=mesh, in_specs=placed, out_specs=P(("img", "row"), "col", None), check_vma=False
    )
```

profile of v0, /device:TPU:0, one launch (start us, length us, event | category | flops | bytes accessed | tf_op | source)
XLA Modules:
  0.0 272.7 jit_solution(14949438277409626070)
XLA Ops:
  6.5 1.3 convert_reduce_fusion
  7.9 0.1 reduce_sum.36
  8.0 0.1 reduce_sum.37
  8.1 34.9 %psum.14 = f32[32]{0:T(128)S(1)} all-reduce(f32[32]{0:T(128)S(1)} %reduce_sum.37), channel_id=1, replica_groups=mesh['img'=2,'row'=4,'col'=4] {'row','col'}, use_global_device_ids=true, to_apply=%region_2.0 | all-reduce | flops 32 | bytes 256 | tf_op jit(solution)/shard_map/psum | solution.py:66
  43.0 0.1 sub.41
  43.1 0.1 sub.42
  43.2 1.3 multiply_reduce_fusion
  44.5 0.1 reduce_sum.47
  44.5 0.1 reduce_sum.48
  44.7 29.5 %psum.15 = f32[32]{0:T(128)S(1)} all-reduce(f32[32]{0:T(128)S(1)} %reduce_sum.48), channel_id=1, replica_groups=mesh['img'=2,'row'=4,'col'=4] {'row','col'}, use_global_device_ids=true, to_apply=%region_5.6 | all-reduce | flops 32 | bytes 256 | tf_op jit(solution)/shard_map/psum | solution.py:69
  74.2 0.1 mul.49
  74.2 0.1 mul.50
  74.3 1.3 fusion.27
  75.7 0.0 copy-start.1
  75.7 3.2 %convolution_convert_fusion = bf16[256,768]{1,0:T(8,128)(2,1)} fusion(bf16[256,1280]{1,0:T(8,128)(2,1)S(1)} %fusion.27, bf16[1280,768]{1,0:T(8,128)(2,1)} %param.15), kind=kOutput, calls=%fused_computation.28 | convolution fusion | flops 503513088 | bytes 3014656 | tf_op jit(solution)/shard_map/dot_general | solution.py:75
  78.9 0.0 all-gather.5.cloned.1.call-update
  78.9 0.0 all-gather.3.cloned.1.call-start
  79.0 3.0 %convolution_convert_fusion.1 = bf16[256,768]{1,0:T(8,128)(2,1)} fusion(bf16[256,1280]{1,0:T(8,128)(2,1)S(1)} %fusion.27, bf16[1280,768]{1,0:T(8,128)(2,1)} %param.14), kind=kOutput, calls=%fused_computation.29 | convolution fusion | flops 503513088 | bytes 3014656 | tf_op jit(solution)/shard_map/dot_general | solution.py:74
  81.9 0.0 all-gather.3.cloned.1.call-update
  82.0 2.5 convolution_convert_fusion.2
  84.5 0.2 copy.18
  84.7 53.5 %all-gather.5.cloned.1.call-done = bf16[4096,768]{1,0:T(8,128)(2,1)} async-done(((bf16[256,768]{1,0:T(8,128)(2,1)}), bf16[4096,768]{1,0:T(8,128)(2,1)}) %all-gather.5.cloned.1.call-update) | async-done | bytes 6291472 | tf_op jit(solution)/shard_map/all_gather | solution.py:80
  138.2 8.8 %copy.20 = bf16[4096,768]{0,1:T(8,128)(2,1)} copy(bf16[4096,768]{1,0:T(8,128)(2,1)} %all-gather.5.cloned.1.call-done) | data formatting | bytes 12582912 | tf_op jit(solution)/shard_map/all_gather | solution.py:80
  146.9 54.0 %all-gather.3.cloned.1.call-done = bf16[4096,768]{1,0:T(8,128)(2,1)} async-done(((bf16[256,768]{1,0:T(8,128)(2,1)}), bf16[4096,768]{1,0:T(8,128)(2,1)}) %all-gather.3.cloned.1.call-update) | async-done | bytes 6291472 | tf_op jit(solution)/shard_map/all_gather | solution.py:79
  200.9 8.6 %copy.19 = bf16[4096,768]{0,1:T(8,128)(2,1)} copy(bf16[4096,768]{1,0:T(8,128)(2,1)} %all-gather.3.cloned.1.call-done) | data formatting | bytes 12582912 | tf_op jit(solution)/shard_map/all_gather | solution.py:79
  209.6 54.7 %while.12 = (s32[]{:T(128)}, f32[12,256]{1,0:T(8,128)S(1)}, f32[12,256,64]{1,2,0:T(8,128)S(1)}, bf16[12,256,64]{1,2,0:T(8,128)(2,1)S(1)}, bf16[12,4096,64]{1,2,0...) while((s32[]{:T(128)}, f32[12,256]{1,0:T(8,128)S(1)}, ...), condition=%wide.region_9.10_spmd, body=%wide.region_6.9_spmd.sunk | while | flops 274744064 | bytes 13745249 | solution.py:32
  209.6 1.9 fusion.44
  211.4 0.7 fusion.45
  212.2 1.9 fusion.46
  214.1 1.9 fusion.44
  216.0 0.7 fusion.45
  216.7 1.9 fusion.46
  218.7 1.9 fusion.44
  220.5 0.7 fusion.45
  221.3 1.9 fusion.46
  223.2 1.9 fusion.44
  225.1 0.7 fusion.45
  225.8 1.9 fusion.46
  227.8 1.9 fusion.44
  229.6 0.7 fusion.45
  230.4 1.9 fusion.46
  232.3 1.9 fusion.44
  234.2 0.7 fusion.45
  234.9 1.9 fusion.46
  236.9 1.9 fusion.44
  238.8 0.7 fusion.45
  239.5 1.9 fusion.46
  241.5 1.9 fusion.44
  243.3 0.7 fusion.45
  244.0 1.9 fusion.46
  246.0 1.9 fusion.44
  247.9 0.7 fusion.45
  248.6 1.9 fusion.46
  250.6 1.9 fusion.44
  252.4 0.7 fusion.45
  253.2 1.9 fusion.46
  255.1 1.9 fusion.44
  257.0 0.7 fusion.45
  257.7 1.9 fusion.46
  259.7 1.9 fusion.44
  261.5 0.7 fusion.45
  262.3 1.9 fusion.46
  264.2 0.1 divide_convert_fusion
  264.3 1.5 fusion.23
  (46 shorter events, 0.7 us)
Async XLA Ops:
  6.5 257.8 %copy-start = (bf16[768,1280]{1,0:T(8,128)(2,1)S(1)}, bf16[768,1280]{1,0:T(8,128)(2,1)}, u32[]{:S(2)}) copy-start(bf16[768,1280]{1,0:T(8,128)(2,1)} %param.16) | copy-start | bytes 5898244
  6.5 131.6 %all-gather.5.cloned.1.call-start = ((), (), s32[]{:S(2)}) async-start(), calls=%async_computation.1 | async-start | bytes 6684672 | tf_op jit(solution)/shard_map/all_gather | solution.py:80
  75.7 6.3 %copy-start.1 = (bf16[256,1280]{1,0:T(8,128)(2,1)}, bf16[256,1280]{1,0:T(8,128)(2,1)S(1)}, u32[]{:S(2)}) copy-start(bf16[256,1280]{1,0:T(8,128)(2,1)S(1)} %fusion.27) | copy-start | bytes 1966084
  78.9 122.0 %all-gather.3.cloned.1.call-start = ((), (), s32[]{:S(2)}) async-start(), calls=%async_computation | async-start | bytes 6684672 | tf_op jit(solution)/shard_map/all_gather | solution.py:79
  209.6 54.8 %copy-start.2 = (f32[1280]{0:T(1024)S(1)}, f32[1280]{0:T(1024)}, u32[]{:S(2)}) copy-start(f32[1280]{0:T(1024)} %param.17) | copy-start | bytes 15364
Sparse Core Ops, SparseCore 0:
  79.0 59.0 all-gather.4
  140.5 60.4 all-gather.2
where the time goes:
time: 275 us; the launch traced here: 273 us
  waiting for transfers between devices  108 us (39%)
  blocking collectives  64.4 us (23%)
  matrix products  55.3 us (20%)
  local copies, waits for them, and re-layouts  18.5 us (7%)
  between operations  13.5 us (5%)
  other arithmetic  13.1 us (5%)
    all_gather x1, waiting for transfers between devices, local(): lax.all_gather(keys, ('row', 'col'), axis=0, tiled=True)  54 us
    all_gather x1, waiting for transfers between devices, local(): lax.all_gather(values, ('row', 'col'), axis=0, tiled=True)  53.5 us
    psum x1, blocking collectives, local(): group_total = lax.psum(jnp.sum(grouped, axis=(0, 2)), ('row', 'col'))  34.9 us
    psum x1, blocking collectives, local(): spread = lax.psum(jnp.sum(centered * centered, axis=(0, 2)), ('row', 'col'))  29.5 us
    dot_general x12, matrix products, per_head(): jnp.dot(rounded, value_one, preferred_element_type=jnp.float32)  22.8 us
    dot_general x12, matrix products, per_head(): jnp.dot(query_one, key_one.T, preferred_element_type=jnp.float32) * scale  22.3 us
    all_gather x1, local copies, waits for them, and re-layouts, local(): lax.all_gather(values, ('row', 'col'), axis=0, tiled=True)  8.75 us
    all_gather x1, local copies, waits for them, and re-layouts, local(): lax.all_gather(keys, ('row', 'col'), axis=0, tiled=True)  8.61 us
  transfers between devices with their start and end apart: 2, of which 2 were waited for; matrix products, arithmetic and copies ran while one was open for 5% of the time, Pallas kernels for 0%

commit v1 on v0

--- a/solution.py
+++ b/solution.py
@@ -63,7 +63,9 @@
     wide = latent.reshape(tok_count, width).astype(jnp.float32)
     grouped = wide.reshape(tok_count, GROUPS, width // GROUPS)
     entries = float(tok_count * lax.axis_size("row") * lax.axis_size("col") * (width // GROUPS))
-    group_total = lax.psum(jnp.sum(grouped, axis=(0, 2)), ("row", "col"))
+    group_total = jnp.sum(grouped, axis=(0, 2))
+    for over in ("col", "row"):
+        group_total = lax.psum(group_total, over)
     mean = group_total / entries
     centered = grouped - mean[None, :, None]
     spread = lax.psum(jnp.sum(centered * centered, axis=(0, 2)), ("row", "col"))

time: 275 us -> 260 us (0.945)
  blocking collectives: 64.4 us -> 49.8 us
    psum x1 -> x2, blocking collectives: 34.9 us -> 20.3 us  [local(): group_total = lax.psum(group_total, over)]
  transfers between devices with their start and end apart: 2 -> 2, of which waited for: 2 -> 2; matrix products, arithmetic and copies ran while one was open for 5% -> 6% of each run, Pallas kernels for 0% -> 0%
where the time goes in v1:
time: 260 us; the launch traced here: 258 us
  waiting for transfers between devices  108 us (42%)
  matrix products  55.3 us (21%)
  blocking collectives  49.8 us (19%)
  local copies, waits for them, and re-layouts  18.5 us (7%)
  between operations  13.5 us (5%)
  other arithmetic  13.1 us (5%)
    all_gather x1, waiting for transfers between devices, local(): lax.all_gather(keys, ('row', 'col'), axis=0, tiled=True)  54 us
    all_gather x1, waiting for transfers between devices, local(): lax.all_gather(values, ('row', 'col'), axis=0, tiled=True)  53.5 us
    psum x1, blocking collectives, local(): spread = lax.psum(jnp.sum(centered * centered, axis=(0, 2)), ('row', 'col'))  29.5 us
    dot_general x12, matrix products, per_head(): jnp.dot(rounded, value_one, preferred_element_type=jnp.float32)  22.8 us
    dot_general x12, matrix products, per_head(): jnp.dot(query_one, key_one.T, preferred_element_type=jnp.float32) * scale  22.3 us
    psum x2, blocking collectives, local(): group_total = lax.psum(group_total, over)  20.3 us
    all_gather x1, local copies, waits for them, and re-layouts, local(): lax.all_gather(values, ('row', 'col'), axis=0, tiled=True)  8.75 us
    all_gather x1, local copies, waits for them, and re-layouts, local(): lax.all_gather(keys, ('row', 'col'), axis=0, tiled=True)  8.61 us
  transfers between devices with their start and end apart: 2, of which 2 were waited for; matrix products, arithmetic and copies ran while one was open for 6% of the time, Pallas kernels for 0%

profile of v1, /device:TPU:0, one launch (start us, length us, event | category | flops | bytes accessed | tf_op | source)
XLA Modules:
  0.0 258.1 jit_solution(5565774108331651904)
XLA Ops:
  6.5 1.3 convert_reduce_fusion
  7.9 0.1 reduce_sum.36
  8.0 0.1 reduce_sum.37
  8.1 8.4 %psum.21 = f32[32]{0:T(128)S(1)} all-reduce(f32[32]{0:T(128)S(1)} %reduce_sum.37), channel_id=1, replica_groups=mesh['img'=2,'row'=4,'col'=4] {'col'}, use_global_device_ids=true, to_apply=%region_2.0 | all-reduce | flops 32 | bytes 256 | tf_op jit(solution)/shard_map/psum | solution.py:68
  16.4 11.9 %psum.22 = f32[32]{0:T(128)S(1)} all-reduce(f32[32]{0:T(128)S(1)} %psum.21), channel_id=1, replica_groups=mesh['img'=2,'row'=4,'col'=4] {'row'}, use_global_device_ids=true, to_apply=%region_3.0 | all-reduce | flops 32 | bytes 256 | tf_op jit(solution)/shard_map/psum | solution.py:68
  28.4 0.1 sub.41
  28.5 0.1 sub.42
  28.6 1.3 multiply_reduce_fusion
  29.8 0.1 reduce_sum.47
  29.9 0.1 reduce_sum.48
  30.1 29.5 %psum.23 = f32[32]{0:T(128)S(1)} all-reduce(f32[32]{0:T(128)S(1)} %reduce_sum.48), channel_id=1, replica_groups=mesh['img'=2,'row'=4,'col'=4] {'row','col'}, use_global_device_ids=true, to_apply=%region_6.7 | all-reduce | flops 32 | bytes 256 | tf_op jit(solution)/shard_map/psum | solution.py:71
  59.6 0.1 mul.49
  59.6 0.1 mul.50
  59.7 1.3 fusion.27
  61.1 3.2 %convolution_convert_fusion = bf16[256,768]{1,0:T(8,128)(2,1)} fusion(bf16[256,1280]{1,0:T(8,128)(2,1)S(1)} %fusion.27, bf16[1280,768]{1,0:T(8,128)(2,1)} %param.15), kind=kOutput, calls=%fused_computation.28 | convolution fusion | flops 503513088 | bytes 3014656 | tf_op jit(solution)/shard_map/dot_general | solution.py:77
  64.3 0.0 all-gather.5.cloned.1.call-update
  64.3 0.0 all-gather.3.cloned.1.call-start
  64.4 3.0 %convolution_convert_fusion.1 = bf16[256,768]{1,0:T(8,128)(2,1)} fusion(bf16[256,1280]{1,0:T(8,128)(2,1)S(1)} %fusion.27, bf16[1280,768]{1,0:T(8,128)(2,1)} %param.14), kind=kOutput, calls=%fused_computation.29 | convolution fusion | flops 503513088 | bytes 3014656 | tf_op jit(solution)/shard_map/dot_general | solution.py:76
  67.3 0.0 all-gather.3.cloned.1.call-update
  67.4 2.5 convolution_convert_fusion.2
  69.9 0.2 copy.18
  70.1 53.5 %all-gather.5.cloned.1.call-done = bf16[4096,768]{1,0:T(8,128)(2,1)} async-done(((bf16[256,768]{1,0:T(8,128)(2,1)}), bf16[4096,768]{1,0:T(8,128)(2,1)}) %all-gather.5.cloned.1.call-update) | async-done | bytes 6291472 | tf_op jit(solution)/shard_map/all_gather | solution.py:82
  123.6 8.8 %copy.20 = bf16[4096,768]{0,1:T(8,128)(2,1)} copy(bf16[4096,768]{1,0:T(8,128)(2,1)} %all-gather.5.cloned.1.call-done) | data formatting | bytes 12582912 | tf_op jit(solution)/shard_map/all_gather | solution.py:82
  132.3 54.0 %all-gather.3.cloned.1.call-done = bf16[4096,768]{1,0:T(8,128)(2,1)} async-done(((bf16[256,768]{1,0:T(8,128)(2,1)}), bf16[4096,768]{1,0:T(8,128)(2,1)}) %all-gather.3.cloned.1.call-update) | async-done | bytes 6291472 | tf_op jit(solution)/shard_map/all_gather | solution.py:81
  186.3 8.6 %copy.19 = bf16[4096,768]{0,1:T(8,128)(2,1)} copy(bf16[4096,768]{1,0:T(8,128)(2,1)} %all-gather.3.cloned.1.call-done) | data formatting | bytes 12582912 | tf_op jit(solution)/shard_map/all_gather | solution.py:81
  194.9 54.7 %while.12 = (s32[]{:T(128)}, f32[12,256]{1,0:T(8,128)S(1)}, f32[12,256,64]{1,2,0:T(8,128)S(1)}, bf16[12,256,64]{1,2,0:T(8,128)(2,1)S(1)}, bf16[12,4096,64]{1,2,0...) while((s32[]{:T(128)}, f32[12,256]{1,0:T(8,128)S(1)}, ...), condition=%wide.region_10.11_spmd, body=%wide.region_7.10_spmd.sunk | while | flops 274744064 | bytes 13745249 | solution.py:32
  194.9 1.9 fusion.44
  196.8 0.7 fusion.45
  197.6 1.9 fusion.46
  199.5 1.9 fusion.44
  201.4 0.7 fusion.45
  202.1 1.9 fusion.46
  204.1 1.9 fusion.44
  205.9 0.7 fusion.45
  206.7 1.9 fusion.46
  208.6 1.9 fusion.44
  210.5 0.7 fusion.45
  211.2 1.9 fusion.46
  213.2 1.9 fusion.44
  215.1 0.7 fusion.45
  215.8 1.9 fusion.46
  217.7 1.9 fusion.44
  219.6 0.7 fusion.45
  220.3 1.9 fusion.46
  222.3 1.9 fusion.44
  224.2 0.7 fusion.45
  224.9 1.9 fusion.46
  226.8 1.9 fusion.44
  228.7 0.7 fusion.45
  229.4 1.9 fusion.46
  231.4 1.9 fusion.44
  233.3 0.7 fusion.45
  234.0 1.9 fusion.46
  236.0 1.9 fusion.44
  237.8 0.7 fusion.45
  238.6 1.9 fusion.46
  240.5 1.9 fusion.44
  242.4 0.7 fusion.45
  243.1 1.9 fusion.46
  245.1 1.9 fusion.44
  246.9 0.7 fusion.45
  247.7 1.9 fusion.46
  249.6 0.1 divide_convert_fusion
  249.7 1.6 fusion.23
  (47 shorter events, 0.8 us)
Async XLA Ops:
  6.5 243.2 %copy-start = (bf16[768,1280]{1,0:T(8,128)(2,1)S(1)}, bf16[768,1280]{1,0:T(8,128)(2,1)}, u32[]{:S(2)}) copy-start(bf16[768,1280]{1,0:T(8,128)(2,1)} %param.16) | copy-start | bytes 5898244
  6.5 117.0 %all-gather.5.cloned.1.call-start = ((), (), s32[]{:S(2)}) async-start(), calls=%async_computation.1 | async-start | bytes 6684672 | tf_op jit(solution)/shard_map/all_gather | solution.py:82
  61.1 6.3 %copy-start.1 = (bf16[256,1280]{1,0:T(8,128)(2,1)}, bf16[256,1280]{1,0:T(8,128)(2,1)S(1)}, u32[]{:S(2)}) copy-start(bf16[256,1280]{1,0:T(8,128)(2,1)S(1)} %fusion.27) | copy-start | bytes 1966084
  64.3 122.0 %all-gather.3.cloned.1.call-start = ((), (), s32[]{:S(2)}) async-start(), calls=%async_computation | async-start | bytes 6684672 | tf_op jit(solution)/shard_map/all_gather | solution.py:81
  194.9 54.8 %copy-start.2 = (f32[1280]{0:T(1024)S(1)}, f32[1280]{0:T(1024)}, u32[]{:S(2)}) copy-start(f32[1280]{0:T(1024)} %param.17) | copy-start | bytes 15364
Sparse Core Ops, SparseCore 0:
  64.4 59.0 all-gather.4
  125.9 60.4 all-gather.2
